TPU v7x, 32 devices: a whole 2x2x4 slice. The times are simulated.
32 devices in a mesh: dp: 8 (over z, y), mp: 4 (over x, core).
Axes of the slice: x: 2, y: 2, z: 4, core: 2. Of those that a mesh axis runs over, the one named last changes fastest.
Arguments:
- tree_query: bfloat16 [1024, 2048], P('dp', 'mp'), may hold values from -6 to 6
- new_kv: bfloat16 [1024, 2, 512], P('dp', None, 'mp'), may hold values from -6 to 6
- kv_cache: bfloat16 [320, 2, 128, 512], P('dp', None, None, 'mp'), may hold values from -4 to 4
- page_table: int32 [16, 32], P('dp'), may hold values from 0 to 39, as said below
- cache_len: int32 [16], P('dp'), may hold values from 2 to 4096, as said below
- tree_mask: int32 [16, 64, 64], P('dp'), may hold values from 0 to 1, as said below
- out_weight: bfloat16 [2048, 2048], P('mp'), may hold values from -0.5 to 0.5
- residual_in: bfloat16 [1024, 2048], P('dp'), may hold values from -3 to 3
- norm_gain: float32 [2048], replicated, may hold values from 0.25 to 1.75
- route_ids: int32 [1024, 6], P('dp'), may hold values from 0 to 7, all different within a row; in each aligned block of 128 rows (0 to 127, 128 to 255, ...) at most 128 rows name the same one
- route_weight: float32 [1024, 6], P('dp'), may hold values from 0.05 to 0.5
- w_gate: bfloat16 [8, 2048, 1408], P('dp', None, 'mp'), may hold values from -0.125 to 0.125
- w_up: bfloat16 [8, 2048, 1408], P('dp', None, 'mp'), may hold values from -0.125 to 0.125
- w_down: bfloat16 [8, 1408, 2048], P('dp', None, 'mp'), may hold values from -0.15625 to 0.15625
- shared_gate: bfloat16 [2048, 2816], P('dp', 'mp'), may hold values from -0.125 to 0.125
- shared_up: bfloat16 [2048, 2816], P('dp', 'mp'), may hold values from -0.125 to 0.125
- shared_down: bfloat16 [2816, 2048], P('mp', 'dp'), may hold values from -0.109375 to 0.109375
Outputs:
- layer_out: bfloat16 [1024, 2048], P('dp', 'mp')
Inputs may be any that keep to these rules, and one draw needn't show every extreme that they name: `route_ids`: each row names 6 different experts. Within the rows of one index of dp (aligned blocks of 128 rows) no expert is named by more than 128 rows, and in some block one expert is named by exactly 128 rows. `cache_len`: the pages of the requests of one index of dp number at most 40 together; some request has exactly 4096 cached positions. `page_table`: entry [r, j] is the slot, in the pool of the index of dp that holds request r, of the page with cache positions j * 128 to j * 128 + 127. Entries with j * 128 < cache_len[r] are distinct over the requests of one index of dp; the other entries are valid slots whose contents are not read. tree_mask[r, i, u] is 1 where tree node u is node i or an ancestor of it, else 0; node 0 is the root and each other node's parent has a smaller index.
All inputs are finite; a program needn't handle non-finite values.
Results may differ from a plain program's by a relative error of at most 0.009.
Values may be sent and summed in bfloat16 or wider, within the bound.
A program may use at most 128 MiB of HBM per device.

v0:
```python
import jax
import jax.numpy as jnp
from jax import lax
from jax.sharding import PartitionSpec as P

NEGATIVE_FILL = -1e30
EPSILON = 1e-05


def normalize(rows, gain):
    values = rows.astype(jnp.float32)
    mean_square = jnp.mean(values * values, axis=-1, keepdims=True)
    return (values * lax.rsqrt(mean_square + EPSILON) * gain).astype(jnp.bfloat16)


def attend_requests(
    queries, tree_keys, tree_values, tree_allow, kv_cache, page_table, cache_len, score_scale
):

    def per_request(request_item):
        q_rows, own_keys, own_values, allow_rows, table_row, length = request_item
        kv_pages = kv_cache[table_row]
        cache_keys = kv_pages[:, 0].reshape(-1, kv_pages.shape[-1])
        cache_values = kv_pages[:, 1].reshape(-1, kv_pages.shape[-1])
        live_mask = (jnp.arange(cache_keys.shape[0], dtype=jnp.int32) < length)[None, :]
        cache_scores = (
            jnp.einsum("qd,kd->qk", q_rows, cache_keys, preferred_element_type=jnp.float32)
            * score_scale
        )
        cache_scores = jnp.where(live_mask, cache_scores, NEGATIVE_FILL)
        tree_scores = (
            jnp.einsum("qd,ud->qu", q_rows, own_keys, preferred_element_type=jnp.float32)
            * score_scale
        )
        tree_scores = jnp.where(allow_rows, tree_scores, NEGATIVE_FILL)
        row_peak = jnp.maximum(jnp.max(cache_scores, axis=1), jnp.max(tree_scores, axis=1))[:, None]
        cache_probs = jnp.where(live_mask, jnp.exp(cache_scores - row_peak), 0.0)
        tree_probs = jnp.where(allow_rows, jnp.exp(tree_scores - row_peak), 0.0)
        denom_sum = jnp.sum(cache_probs, axis=1) + jnp.sum(tree_probs, axis=1)
        weighted = jnp.dot(
            cache_probs.astype(jnp.bfloat16), cache_values, preferred_element_type=jnp.float32
        )
        weighted = weighted + jnp.dot(
            tree_probs.astype(jnp.bfloat16), own_values, preferred_element_type=jnp.float32
        )
        return (weighted / denom_sum[:, None]).astype(jnp.bfloat16)

    return lax.map(
        per_request, (queries, tree_keys, tree_values, tree_allow, page_table, cache_len)
    )


def run_experts(rows, w_gate, w_up, w_down):
    source_count, slot_count, model_width = rows.shape
    flat_rows = rows.reshape(source_count * slot_count, model_width)
    gate_proj = jnp.dot(flat_rows, w_gate[0], preferred_element_type=jnp.float32)
    up_proj = jnp.dot(flat_rows, w_up[0], preferred_element_type=jnp.float32)
    hidden_act = (jax.nn.silu(gate_proj) * up_proj).astype(jnp.bfloat16)
    down_rows = w_down[0]
    summed = jnp.dot(
        lax.all_gather(hidden_act, "mp", axis=1, tiled=True),
        down_rows,
        preferred_element_type=jnp.float32,
    )
    outputs = summed.astype(jnp.bfloat16).reshape(source_count, slot_count, w_down.shape[2])
    return lax.all_to_all(outputs, "dp", split_axis=0, concat_axis=0, tiled=True)


def shared_experts(normed_rows, shared_gate, shared_up, shared_down):
    gate_total = jnp.dot(
        normed_rows,
        lax.all_gather(shared_gate, "dp", axis=0, tiled=True),
        preferred_element_type=jnp.float32,
    )
    up_total = jnp.dot(
        normed_rows,
        lax.all_gather(shared_up, "dp", axis=0, tiled=True),
        preferred_element_type=jnp.float32,
    )
    shared_hidden = (jax.nn.silu(gate_total) * up_total).astype(jnp.bfloat16)
    terms = jnp.dot(
        shared_hidden,
        lax.all_gather(shared_down, "dp", axis=1, tiled=True),
        preferred_element_type=jnp.float32,
    )
    return lax.psum_scatter(terms.astype(jnp.bfloat16), "mp", scatter_dimension=1, tiled=True)


def on_device(
    tree_query,
    new_kv,
    kv_cache,
    page_table,
    cache_len,
    tree_mask,
    out_weight,
    residual_in,
    norm_gain,
    route_ids,
    route_weight,
    w_gate,
    w_up,
    w_down,
    shared_gate,
    shared_up,
    shared_down,
):
    tok_rows = tree_query.shape[0]
    req_count = cache_len.shape[0]
    tree_len = tree_mask.shape[1]
    head_width = new_kv.shape[2]
    local_heads = tree_query.shape[1] // head_width
    score_scale = head_width ** (-0.5)
    queries = tree_query.reshape(req_count, tree_len, local_heads, head_width)
    queries = queries.transpose(0, 2, 1, 3).reshape(req_count, local_heads * tree_len, head_width)
    tree_keys = new_kv[:, 0, :].reshape(req_count, tree_len, head_width)
    tree_values = new_kv[:, 1, :].reshape(req_count, tree_len, head_width)
    tree_allow = jnp.tile(tree_mask, (1, local_heads, 1)) == 1
    attended = attend_requests(
        queries, tree_keys, tree_values, tree_allow, kv_cache, page_table, cache_len, score_scale
    )
    attended = attended.reshape(req_count, local_heads, tree_len, head_width).transpose(0, 2, 1, 3)
    attended = attended.reshape(tok_rows, local_heads * head_width)
    partial_value = jnp.dot(attended, out_weight, preferred_element_type=jnp.float32)
    model_width = residual_in.shape[1]
    quarter = model_width // lax.axis_size("mp")
    col_start = lax.axis_index("mp") * quarter
    experts = lax.axis_size("dp") * w_gate.shape[0]
    route_count = route_ids.shape[1]
    capacity = min(tok_rows, 4 * tok_rows * route_count // (3 * experts))
    expert_ids = route_ids.reshape(-1)
    onehot = (expert_ids[:, None] == jnp.arange(experts, dtype=jnp.int32)[None, :]).astype(
        jnp.int32
    )
    slot_index = jnp.sum((jnp.cumsum(onehot, axis=0) - onehot) * onehot, axis=1)
    sources = jnp.arange(expert_ids.shape[0], dtype=jnp.int32) // route_count
    summed_heads = lax.psum(partial_value, "mp")
    stream = (residual_in.astype(jnp.float32) + summed_heads).astype(jnp.bfloat16)
    own_stream = lax.dynamic_slice_in_dim(stream, col_start, quarter, 1)
    normed_rows = normalize(stream, norm_gain)
    buffer = jnp.zeros((experts, capacity, normed_rows.shape[1]), jnp.bfloat16)
    results = run_experts(
        lax.all_to_all(
            buffer.at[expert_ids, slot_index].set(normed_rows[sources]),
            "dp",
            split_axis=0,
            concat_axis=0,
            tiled=True,
        ),
        w_gate,
        w_up,
        w_down,
    )
    shared_out = shared_experts(normed_rows, shared_gate, shared_up, shared_down)
    result_rows = results.reshape(experts * capacity, quarter)
    picked = (
        result_rows[expert_ids * capacity + slot_index]
        .reshape(tok_rows, route_count, quarter)
        .astype(jnp.float32)
    )
    mixture = jnp.einsum("tk,tkc->tc", route_weight, picked, precision=lax.Precision.HIGHEST)
    return (own_stream.astype(jnp.float32) + shared_out.astype(jnp.float32) + mixture).astype(
        jnp.bfloat16
    )


def solution(mesh):
    return jax.shard_map(
        on_device,
        mesh=mesh,
        in_specs=(
            P("dp", "mp"),
            P("dp", None, "mp"),
            P("dp", None, None, "mp"),
            P("dp", None),
            P("dp"),
            P("dp", None, None),
            P("mp", None),
            P("dp", None),
            P(),
            P("dp", None),
            P("dp", None),
            P("dp", None, "mp"),
            P("dp", None, "mp"),
            P("dp", None, "mp"),
            P("dp", "mp"),
            P("dp", "mp"),
            P("mp", "dp"),
        ),
        out_specs=P("dp", "mp"),
        check_vma=False,
    )
```

profile of v0, /device:TPU:13, one launch (start us, length us, event | category | flops | bytes accessed | tf_op | source)
XLA Modules:
  0.0 579.2 jit_solution(8507746179969428478)
XLA Ops:
  6.5 1.1 fusion.65
  7.7 0.9 reshape.211
  9.9 21.6 %while.10 = (s32[]{:T(128)}, bf16[2,256,128]{2,1,0:T(8,128)(2,1)S(1)}, s32[2]{0:T(128)}, bf16[2,256,128]{2,1,0:T(8,128)(2,1)S(1)}, s32[2,32]{1,0:T(2,128)}, /*in...) while((s32[]{:T(128)}, ...), condition=%wide.region_5.6_spmd, body=%wide.region_0.5_spmd.sunk | while | flops 554947200 | bytes 23845564 | solution.py:48
  10.6 3.9 gather_fusion
  14.5 1.7 fusion.100
  18.6 0.9 fusion.104
  21.4 3.9 gather_fusion
  25.3 1.7 fusion.100
  29.4 0.9 fusion.104
  31.7 1.5 fusion.51
  33.8 1.7 reduce-window.6
  36.1 34.0 %all-reduce.2.cloned.1.call-done = f32[128,2048]{1,0:T(8,128)} async-done(((f32[128,2048]{1,0:T(8,128)}), f32[128,2048]{1,0:T(8,128)}) %all-reduce.2.cloned.1.call-update) | async-done | bytes 1048592 | tf_op jit(solution)/shard_map/psum | solution.py:137
  70.1 1.5 fusion.41
  72.6 4.3 gather_fusion.1
  76.9 2.4 broadcast_in_dim.47
  79.3 137.5 %scatter_fusion = bf16[8,128,2048]{2,1,0:T(8,128)(2,1)} fusion(bf16[8,128,2048]{2,1,0:T(8,128)(2,1)} %broadcast_in_dim.47, s32[768]{0:T(1024)S(1)} %get-tuple-element.54, bf16[768,2048]{1,0:T(8,128)(2,1)} %gather_fusion.1), kind=kCustom, calls=%fused_computation.3 | custom fusion | bytes 9443328 | tf_op jit(solution)/shard_map/scatter | solution.py:144
  216.8 95.4 %all_to_all.10 = bf16[8,128,2048]{2,1,0:T(8,128)(2,1)S(1)} all-to-all(bf16[8,128,2048]{2,1,0:T(8,128)(2,1)} %scatter_fusion), channel_id=1, replica_groups=mesh['dp'=8,'mp'=4] {'dp'}, dimensions={0} | all-to-all | bytes 8388608 | tf_op jit(solution)/shard_map/all_to_all | solution.py:143
  312.3 1.7 fusion.35
  314.0 2.7 fusion.37
  318.7 27.8 %all-gather.11.cloned.1.call-done = bf16[1024,1408]{0,1:T(8,128)(2,1)} async-done(((bf16[1024,352]{0,1:T(8,128)(2,1)}), bf16[1024,1408]{0,1:T(8,128)(2,1)}) %all-gather.11.cloned.1.call-update) | async-done | bytes 2883600 | tf_op jit(solution)/shard_map/all_gather | solution.py:61
  346.4 5.0 convolution_convert_fusion.1
  351.5 5.5 all-to-all-start.1
  357.0 64.3 %all-gather.5.cloned.1.call-done = bf16[2048,704]{0,1:T(8,128)(2,1)} async-done(((bf16[256,704]{0,1:T(8,128)(2,1)}), bf16[2048,704]{0,1:T(8,128)(2,1)}) %all-gather.5.cloned.1.call-update) | async-done | bytes 2883600 | tf_op jit(solution)/shard_map/all_gather | solution.py:72
  421.3 2.7 fusion.66
  424.0 57.6 %all-gather.7.cloned.1.call-done = bf16[2048,704]{0,1:T(8,128)(2,1)} async-done(((bf16[256,704]{0,1:T(8,128)(2,1)}), bf16[2048,704]{0,1:T(8,128)(2,1)}) %all-gather.7.cloned.1.call-update) | async-done | bytes 2883600 | tf_op jit(solution)/shard_map/all_gather | solution.py:77
  481.6 60.3 %all-gather.9.cloned.1.call-done = bf16[704,2048]{1,0:T(8,128)(2,1)} async-done(((bf16[704,256]{1,0:T(8,128)(2,1)}), bf16[704,2048]{1,0:T(8,128)(2,1)}) %all-gather.9.cloned.1.call-update) | async-done | bytes 2883600 | tf_op jit(solution)/shard_map/all_gather | solution.py:83
  542.0 5.6 convolution_convert_fusion
  547.8 4.7 gather_fusion.2
  552.5 1.3 reshape.220
  553.8 1.0 fusion.67
  554.8 15.9 %reduce-scatter.2.cloned.1.call-done = bf16[128,512]{1,0:T(8,128)(2,1)} async-done(((bf16[128,2048]{1,0:T(8,128)(2,1)}), bf16[128,512]{1,0:T(8,128)(2,1)}) %reduce-scatter.2.cloned.1.call-update) | async-done | bytes 131088 | tf_op jit(solution)/shard_map/reduce_scatter | solution.py:86
  570.7 1.7 fusion.49
  (81 shorter events, 14.0 us)
Async XLA Ops:
  6.5 25.1 %copy-start = (bf16[512,2048]{1,0:T(8,128)(2,1)S(1)}, bf16[512,2048]{1,0:T(8,128)(2,1)}, u32[]{:S(2)}) copy-start(bf16[512,2048]{1,0:T(8,128)(2,1)} %param.25) | copy-start | bytes 6291460
  6.5 63.5 %all-reduce.2.cloned.1.call-start = ((), (), s32[]{:S(2)}) async-start(), calls=%async_computation.3 | async-start | bytes 2097152 | tf_op jit(solution)/shard_map/psum | solution.py:137
  14.5 1.7 copy-start.8
  25.3 1.7 copy-start.8
  31.5 1.7 copy-start.4
  31.5 38.6 %copy-start.2 = (bf16[128,2048]{1,0:T(8,128)(2,1)S(1)}, bf16[128,2048]{1,0:T(8,128)(2,1)}, u32[]{:S(2)}) copy-start(bf16[128,2048]{1,0:T(8,128)(2,1)} %param.26) | copy-start | bytes 1572868
  31.6 40.8 %copy-start.3 = (f32[2048]{0:T(1024)S(1)}, f32[2048]{0:T(1024)}, u32[]{:S(2)}) copy-start(f32[2048]{0:T(1024)} %param.27) | copy-start | bytes 24580
  33.2 313.3 %all-gather.11.cloned.1.call-start = ((), (), s32[]{:S(2)}) async-start(), calls=%async_computation.8 | async-start | bytes 3604480 | tf_op jit(solution)/shard_map/all_gather | solution.py:61
  71.6 0.8 copy-start.1
  216.8 95.4 %copy-start.6 = (bf16[1,2048,352]{1,2,0:T(8,128)(2,1)S(1)}, bf16[1,2048,352]{1,2,0:T(8,128)(2,1)}, u32[]{:S(2)}) copy-start(bf16[1,2048,352]{1,2,0:T(8,128)(2,1)} %param.30) | copy-start | bytes 4325380
  312.3 1.8 copy-start.7
  316.8 104.5 %all-gather.5.cloned.1.call-start = ((), (), s32[]{:S(2)}) async-start(), calls=%async_computation.4 | async-start | bytes 3244032 | tf_op jit(solution)/shard_map/all_gather | solution.py:72
  317.5 164.1 %all-gather.7.cloned.1.call-start = ((), (), s32[]{:S(2)}) async-start(), calls=%async_computation.5 | async-start | bytes 3244032 | tf_op jit(solution)/shard_map/all_gather | solution.py:77
  318.1 223.9 %all-gather.9.cloned.1.call-start = ((), (), s32[]{:S(2)}) async-start(), calls=%async_computation.6 | async-start | bytes 3244032 | tf_op jit(solution)/shard_map/all_gather | solution.py:83
  351.5 196.3 %all-to-all-start.1 = ((bf16[8,128,512]{2,1,0:T(8,128)(2,1)}), bf16[8,128,512]{2,1,0:T(8,128)(2,1)}, u32[]{:S(2)}, u32[]{:S(2)}) async-start(bf16[8,128,512]{2,1,0:T(8,128)(2,1)} %bitcast.129), calls=%async_computation.2 | async-start | bytes 2097152 | tf_op jit(solution)/shard_map/all_to_all | solution.py:66
  357.0 213.8 %reduce-scatter.2.cloned.1.call-start = ((), (), s32[]{:S(2)}) async-start(), calls=%async_computation.7 | async-start | bytes 655360 | tf_op jit(solution)/shard_map/reduce_scatter | solution.py:86
  424.0 123.6 %copy-start.5 = (f32[128,6]{0,1:T(8,128)S(1)}, f32[128,6]{0,1:T(8,128)}, u32[]{:S(2)}) copy-start(f32[128,6]{0,1:T(8,128)} %param.29) | copy-start | bytes 9220
Sparse Core Ops, SparseCore 0:
  33.3 36.7 all-reduce.1
  316.9 29.5 all-gather.10
  348.7 72.5 all-gather.4
  423.4 58.1 all-gather.6
  483.7 58.1 all-gather.8
  547.7 22.9 reduce-scatter.1
where the time goes:
time: 584 us; the launch traced here: 579 us
  waiting for transfers between devices  262 us (45%)
  local copies, waits for them, and re-layouts  167 us (29%)
  blocking collectives  95.4 us (16%)
  matrix products  24.5 us (4%)
  between operations  13.7 us (2%)
  other arithmetic  10.9 us (2%)
    scatter x1, local copies, waits for them, and re-layouts, on_device(): buffer.at[expert_ids, slot_index].set(normed_rows[sources])  138 us
    all_to_all x1, blocking collectives, on_device(): lax.all_to_all(buffer.at[expert_ids, slot_index].set(normed_rows[sources]...  95.4 us
    all_gather x1, waiting for transfers between devices, shared_experts(): lax.all_gather(shared_gate, 'dp', axis=0, tiled=True)  64.3 us
    all_gather x1, waiting for transfers between devices, shared_experts(): lax.all_gather(shared_down, 'dp', axis=1, tiled=True)  60.3 us
    all_gather x1, waiting for transfers between devices, shared_experts(): lax.all_gather(shared_up, 'dp', axis=0, tiled=True)  57.6 us
    psum x1, waiting for transfers between devices, on_device(): summed_heads = lax.psum(partial_value, 'mp')  34 us
    all_gather x1, waiting for transfers between devices, run_experts(): lax.all_gather(hidden_act, 'mp', axis=1, tiled=True)  27.8 us
    reduce_scatter x1, waiting for transfers between devices, shared_experts(): lax.psum_scatter(terms.astype(jnp.bfloat16), 'mp', scatter_dimension=1, t...  15.9 us
  transfers between devices with their start and end apart: 7, of which 6 were waited for; matrix products, arithmetic and copies ran while one was open for 4% of the time, Pallas kernels for 0%

commit v1 on v0

v1 whole, which is shorter than its diff:
```python
import functools

import jax
import jax.numpy as jnp
from jax import lax
from jax.experimental import pallas as pl
from jax.experimental.pallas import tpu as pltpu
from jax.sharding import PartitionSpec as P

MESH = pl.DeviceIdType.MESH

NEGATIVE_FILL = -1e30
EPSILON = 1e-05
LOG2_E = 1.4426950408889634


def normalize(rows, gain):
    values = rows.astype(jnp.float32)
    mean_square = jnp.mean(values * values, axis=-1, keepdims=True)
    return (values * lax.rsqrt(mean_square + EPSILON) * gain).astype(jnp.bfloat16)


def attend_kernel(
    heads,
    group,
    score_scale,
    table_ref,
    length_ref,
    query_ref,
    fresh_ref,
    mask_ref,
    cache_ref,
    weight_ref,
    out_ref,
    attended,
):
    req_count, tree_len = mask_ref.shape[0], mask_ref.shape[1]
    page, dim = cache_ref.shape[2], cache_ref.shape[3]
    factor = score_scale * LOG2_E
    contract = (((1,), (1,)), ((), ()))
    for r in range(req_count):
        tokens = slice(r * tree_len, (r + 1) * tree_len)
        queries = jnp.concatenate(
            [query_ref[tokens, h * dim : (h + 1) * dim] for h in range(heads)], axis=0
        )
        allow = jnp.concatenate([mask_ref[r]] * heads, axis=0) == 1
        scores = (
            lax.dot_general(
                queries, fresh_ref[tokens, :dim], contract, preferred_element_type=jnp.float32
            )
            * factor
        )
        scores = jnp.where(allow, scores, NEGATIVE_FILL)
        peak = jnp.max(scores, axis=1, keepdims=True)
        probs = jnp.where(allow, jnp.exp2(scores - peak), 0.0)
        denom = jnp.sum(probs, axis=1, keepdims=True)
        weighted = jnp.dot(
            probs.astype(jnp.bfloat16),
            fresh_ref[tokens, dim:],
            preferred_element_type=jnp.float32,
        )
        length = length_ref[r]

        def step(j, carry):
            peak, denom, weighted = carry
            slots = [table_ref[r, j * group + i] for i in range(group)]
            keys = jnp.concatenate([cache_ref[slot, 0] for slot in slots], axis=0)
            values = jnp.concatenate([cache_ref[slot, 1] for slot in slots], axis=0)
            scores = (
                lax.dot_general(queries, keys, contract, preferred_element_type=jnp.float32)
                * factor
            )
            places = lax.broadcasted_iota(jnp.int32, (1, group * page), 1) + j * (group * page)
            scores = jnp.where(places < length, scores, NEGATIVE_FILL)
            new_peak = jnp.maximum(peak, jnp.max(scores, axis=1, keepdims=True))
            probs = jnp.exp2(scores - new_peak)
            shrink = jnp.exp2(peak - new_peak)
            denom = denom * shrink + jnp.sum(probs, axis=1, keepdims=True)
            weighted = weighted * shrink + jnp.dot(
                probs.astype(jnp.bfloat16), values, preferred_element_type=jnp.float32
            )
            return new_peak, denom, weighted

        steps = (length + group * page - 1) // (group * page)
        peak, denom, weighted = lax.fori_loop(0, steps, step, (peak, denom, weighted))
        result = (weighted / denom).astype(jnp.bfloat16)
        for h in range(heads):
            attended[tokens, h * dim : (h + 1) * dim] = result[h * tree_len : (h + 1) * tree_len]
    out_ref[...] = jnp.dot(
        attended[...], weight_ref[...], preferred_element_type=jnp.float32
    ).astype(out_ref.dtype)


def attend(
    tree_query, new_kv, kv_cache, page_table, cache_len, tree_mask, out_weight, out_dtype
):
    tok_rows, dim = tree_query.shape[0], new_kv.shape[2]
    heads = tree_query.shape[1] // dim
    group = 4 if page_table.shape[1] % 4 == 0 else 1
    vmem, smem = pl.BlockSpec(memory_space=pltpu.VMEM), pl.BlockSpec(memory_space=pltpu.SMEM)
    return pl.pallas_call(
        functools.partial(attend_kernel, heads, group, dim ** (-0.5)),
        out_shape=jax.ShapeDtypeStruct((tok_rows, out_weight.shape[1]), out_dtype),
        in_specs=[smem, smem, vmem, vmem, vmem, vmem, vmem],
        out_specs=vmem,
        scratch_shapes=[pltpu.VMEM(tree_query.shape, jnp.bfloat16)],
        compiler_params=pltpu.CompilerParams(vmem_limit_bytes=24 * 1024 * 1024),
        cost_estimate=pl.CostEstimate(
            flops=1_000_000_000, bytes_accessed=6_000_000, transcendentals=1_200_000
        ),
        name="attend",
    )(
        page_table,
        cache_len,
        tree_query,
        new_kv.reshape(tok_rows, 2 * dim),
        tree_mask,
        kv_cache,
        out_weight,
    )


def run_experts(rows, w_gate, w_up, w_down):
    source_count, slot_count, model_width = rows.shape
    flat_rows = rows.reshape(source_count * slot_count, model_width)
    gate_proj = jnp.dot(flat_rows, w_gate[0], preferred_element_type=jnp.float32)
    up_proj = jnp.dot(flat_rows, w_up[0], preferred_element_type=jnp.float32)
    hidden_act = (jax.nn.silu(gate_proj) * up_proj).astype(jnp.bfloat16)
    down_rows = w_down[0]
    summed = jnp.dot(
        lax.all_gather(hidden_act, "mp", axis=1, tiled=True),
        down_rows,
        preferred_element_type=jnp.float32,
    )
    outputs = summed.astype(jnp.bfloat16).reshape(source_count, slot_count, w_down.shape[2])
    return lax.all_to_all(outputs, "dp", split_axis=0, concat_axis=0, tiled=True)


def shared_experts(normed_rows, shared_gate, shared_up, shared_down):
    gate_total = jnp.dot(
        normed_rows,
        lax.all_gather(shared_gate, "dp", axis=0, tiled=True),
        preferred_element_type=jnp.float32,
    )
    up_total = jnp.dot(
        normed_rows,
        lax.all_gather(shared_up, "dp", axis=0, tiled=True),
        preferred_element_type=jnp.float32,
    )
    shared_hidden = (jax.nn.silu(gate_total) * up_total).astype(jnp.bfloat16)
    terms = jnp.dot(
        shared_hidden,
        lax.all_gather(shared_down, "dp", axis=1, tiled=True),
        preferred_element_type=jnp.float32,
    )
    return lax.psum_scatter(terms.astype(jnp.bfloat16), "mp", scatter_dimension=1, tiled=True)


def mp_relations(m):
    x, c = m // 2, m % 2
    return (x * 2 + (1 - c), (1 - x) * 2 + c, (1 - x) * 2 + (1 - c))


def remote(src, dst, send, recv, device):
    return pltpu.make_async_remote_copy(
        src_ref=src, dst_ref=dst, send_sem=send, recv_sem=recv, device_id=device, device_id_type=MESH
    )


def greet(devices):
    barrier = pltpu.get_barrier_semaphore()
    for device in devices:
        pl.semaphore_signal(barrier, inc=1, device_id=device, device_id_type=MESH)
    pl.semaphore_wait(barrier, len(devices))


def norm_gather_kernel(
    n_dp,
    partial_ref,
    residual_ref,
    gain_ref,
    rows_ref,
    stream_ref,
    terms,
    stream_own,
    normed_own,
    rs_send,
    rs_recv,
    st_send,
    st_recv,
    dp_send,
    dp_recv,
    x_send,
    x_recv,
    c_send,
    c_recv,
    r_send,
    r_recv,
    local_sem,
):
    d, m = lax.axis_index("dp"), lax.axis_index("mp")
    mates = mp_relations(m)
    core_mate, x_mate = mates[0], mates[1]
    peers = [lax.rem(d + k, n_dp) for k in range(1, n_dp)]
    greet([(d, mate) for mate in mates] + [(peer, m) for peer in peers])
    quarter = stream_own.shape[2]
    rs_copies = [
        remote(partial_ref.at[mate], terms.at[i], rs_send.at[i], rs_recv.at[i], (d, mate))
        for i, mate in enumerate(mates)
    ]
    for copy in (rs_copies[1], rs_copies[2], rs_copies[0]):
        copy.start()
    total = residual_ref[...].astype(jnp.float32) + partial_ref[m].astype(jnp.float32)
    for i, copy in enumerate(rs_copies):
        copy.wait_recv()
        total = total + terms[i].astype(jnp.float32)
    stream = total.astype(jnp.bfloat16)
    values = stream.astype(jnp.float32)
    mean_square = jnp.mean(values * values, axis=-1, keepdims=True)
    normed_own[...] = (values * lax.rsqrt(mean_square + EPSILON) * gain_ref[...]).astype(
        jnp.bfloat16
    )
    for i in range(4):
        stream_own[i] = stream[:, i * quarter : (i + 1) * quarter]
    dp_copies = [
        remote(normed_own, rows_ref.at[d, m], dp_send.at[k], dp_recv.at[k], (peers[k], m))
        for k in range(n_dp - 1)
    ]
    for copy in dp_copies:
        copy.start()
    x_copies, c_copies, r_copies = [], [], []

    def forward(k, source):
        owner = lax.rem(d + n_dp - k, n_dp)
        x_copy = remote(source, rows_ref.at[owner, m], x_send.at[k], x_recv.at[k], (d, x_mate))
        c_copy = remote(source, rows_ref.at[owner, m], c_send.at[k], c_recv.at[k], (d, core_mate))
        x_copy.start()
        c_copy.start()
        x_copies.append(x_copy)
        c_copies.append(c_copy)

    def relay(k):
        owner = lax.rem(d + n_dp - k, n_dp)
        x_copies[k].wait_recv()
        block = rows_ref.at[owner, x_mate]
        copy = remote(block, block, r_send.at[k], r_recv.at[k], (d, core_mate))
        copy.start()
        r_copies.append(copy)

    forward(0, normed_own)
    own_rows = pltpu.make_async_copy(normed_own, rows_ref.at[d, m], local_sem.at[0])
    own_rows.start()
    own_stream = pltpu.make_async_copy(stream_own.at[m], stream_ref.at[m], local_sem.at[1])
    own_stream.start()
    st_copies = [
        remote(stream_own.at[mate], stream_ref.at[m], st_send.at[i], st_recv.at[i], (d, mate))
        for i, mate in enumerate(mates)
    ]
    for copy in st_copies:
        copy.start()
    for k in range(1, n_dp):
        dp_copies[k - 1].wait_recv()
        forward(k, rows_ref.at[lax.rem(d + n_dp - k, n_dp), m])
        relay(k - 1)
    relay(n_dp - 1)
    own_rows.wait()
    own_stream.wait()
    for copy in rs_copies + dp_copies + x_copies:
        copy.wait_send()
    for copy in st_copies + c_copies + r_copies:
        copy.wait()


def norm_gather(n_dp, partial, residual, gain):
    rows, width = residual.shape
    dma = pltpu.SemaphoreType.DMA
    return pl.pallas_call(
        functools.partial(norm_gather_kernel, n_dp),
        out_shape=(
            jax.ShapeDtypeStruct((n_dp, 4, rows, width), jnp.bfloat16),
            jax.ShapeDtypeStruct((4, rows, width // 4), jnp.bfloat16),
        ),
        in_specs=[pl.BlockSpec(memory_space=pltpu.VMEM)] * 3,
        out_specs=(pl.BlockSpec(memory_space=pl.ANY),) * 2,
        scratch_shapes=[
            pltpu.VMEM((3, rows, width), jnp.bfloat16),
            pltpu.VMEM((4, rows, width // 4), jnp.bfloat16),
            pltpu.VMEM((rows, width), jnp.bfloat16),
            dma((3,)),
            dma((3,)),
            dma((3,)),
            dma((3,)),
            dma((n_dp - 1,)),
            dma((n_dp - 1,)),
            dma((n_dp,)),
            dma((n_dp,)),
            dma((n_dp,)),
            dma((n_dp,)),
            dma((n_dp,)),
            dma((n_dp,)),
            dma((2,)),
        ],
        compiler_params=pltpu.CompilerParams(
            collective_id=0, has_side_effects=True, vmem_limit_bytes=16 * 1024 * 1024
        ),
        name="norm_gather",
    )(partial, residual, gain)


def hidden_gather_kernel(
    chunks, own_ref, all_ref, x_send, x_recv, c_send, c_recv, r_send, r_recv, local_sem
):
    d, m = lax.axis_index("dp"), lax.axis_index("mp")
    core_mate, x_mate, _ = mp_relations(m)
    greet([(d, core_mate), (d, x_mate)])
    x_copies = [
        remote(own_ref.at[k], all_ref.at[m, k], x_send.at[k], x_recv.at[k], (d, x_mate))
        for k in range(chunks)
    ]
    c_copies = [
        remote(own_ref.at[k], all_ref.at[m, k], c_send.at[k], c_recv.at[k], (d, core_mate))
        for k in range(chunks)
    ]
    for copy in x_copies + c_copies:
        copy.start()
    local = pltpu.make_async_copy(own_ref, all_ref.at[m], local_sem)
    local.start()
    r_copies = []
    for k in range(chunks):
        x_copies[k].wait_recv()
        block = all_ref.at[x_mate, k]
        copy = remote(block, block, r_send.at[k], r_recv.at[k], (d, core_mate))
        copy.start()
        r_copies.append(copy)
    local.wait()
    for copy in x_copies:
        copy.wait_send()
    for copy in c_copies + r_copies:
        copy.wait()


def hidden_gather(own):
    chunks, rows, width = own.shape
    return pl.pallas_call(
        functools.partial(hidden_gather_kernel, chunks),
        out_shape=jax.ShapeDtypeStruct((4, chunks, rows, width), own.dtype),
        in_specs=[pl.BlockSpec(memory_space=pl.ANY)],
        out_specs=pl.BlockSpec(memory_space=pl.ANY),
        scratch_shapes=[pltpu.SemaphoreType.DMA((chunks,))] * 6 + [pltpu.SemaphoreType.DMA],
        compiler_params=pltpu.CompilerParams(collective_id=1, has_side_effects=True),
        name="hidden_gather",
    )(own)


def combine_kernel(n_dp, own_ref, all_ref, send, recv, local_sem):
    d, m = lax.axis_index("dp"), lax.axis_index("mp")
    peers = [lax.rem(d + k, n_dp) for k in range(1, n_dp)]
    greet([(peer, m) for peer in peers])
    copies = [
        remote(own_ref.at[peers[k]], all_ref.at[d], send.at[k], recv.at[k], (peers[k], m))
        for k in range(n_dp - 1)
    ]
    for copy in copies:
        copy.start()
    local = pltpu.make_async_copy(own_ref.at[d], all_ref.at[d], local_sem)
    local.start()
    local.wait()
    for copy in copies:
        copy.wait()


def combine(own):
    n_dp = own.shape[0]
    return pl.pallas_call(
        functools.partial(combine_kernel, n_dp),
        out_shape=jax.ShapeDtypeStruct(own.shape, own.dtype),
        in_specs=[pl.BlockSpec(memory_space=pl.ANY)],
        out_specs=pl.BlockSpec(memory_space=pl.ANY),
        scratch_shapes=[pltpu.SemaphoreType.DMA((n_dp - 1,))] * 2 + [pltpu.SemaphoreType.DMA],
        compiler_params=pltpu.CompilerParams(collective_id=2, has_side_effects=True),
        name="combine",
    )(own)


def shared_slices(shared_gate, shared_up, shared_down):
    n_dp = lax.axis_size("dp")
    depth, units = shared_gate.shape
    share = units // n_dp
    parts = jnp.concatenate(
        [
            shared_gate.T.reshape(n_dp, share, depth),
            shared_up.T.reshape(n_dp, share, depth),
            shared_down.reshape(n_dp, share, depth),
        ],
        axis=1,
    )
    parts = lax.all_to_all(parts, "dp", split_axis=0, concat_axis=0, tiled=True)
    parts = parts.transpose(1, 0, 2).reshape(3, share, n_dp * depth)
    down = parts[2].reshape(share, 4, -1).transpose(1, 0, 2)
    down = lax.all_to_all(down, "mp", split_axis=0, concat_axis=0, tiled=True)
    return parts[0].T, parts[1].T, down


def dense_tail(
    partial_value,
    residual_in,
    norm_gain,
    route_ids,
    route_weight,
    w_gate,
    w_up,
    w_down,
    shared_gate,
    shared_up,
    shared_down,
):
    n_dp = lax.axis_size("dp")
    tok_rows, model_width = residual_in.shape
    units = w_gate.shape[2]
    own_gate, own_up, own_down = shared_slices(shared_gate, shared_up, shared_down)
    share = own_gate.shape[1]
    width = -(-(units + share) // 128) * 128
    spare = width - units - share
    columns_pad = jnp.zeros((model_width, spare), jnp.bfloat16)
    gate_all = jnp.concatenate([w_gate[0], own_gate, columns_pad], axis=1)
    up_all = jnp.concatenate([w_up[0], own_up, columns_pad], axis=1)
    down_width = w_down.shape[2]
    down_all = jnp.concatenate(
        [
            w_down[0].reshape(4, units, down_width),
            own_down,
            jnp.zeros((4, spare, down_width), jnp.bfloat16),
        ],
        axis=1,
    ).reshape(4 * width, down_width)
    chosen = route_ids[None, :, :] == jnp.arange(n_dp, dtype=jnp.int32)[:, None, None]
    by_expert = jnp.sum(jnp.where(chosen, route_weight[None], 0.0), axis=2)
    row_scale = lax.all_to_all(by_expert, "dp", split_axis=0, concat_axis=0, tiled=True)
    row_scale = row_scale.reshape(n_dp * tok_rows, 1)
    slice_rows = tok_rows // 4
    own_start = lax.axis_index("mp") * slice_rows
    rows, stream = norm_gather(
        n_dp,
        partial_value.reshape(4, slice_rows, model_width),
        lax.dynamic_slice_in_dim(residual_in, own_start, slice_rows, 0),
        norm_gain.reshape(1, model_width),
    )
    rows = rows.reshape(n_dp * tok_rows, model_width)
    gate_proj = jnp.dot(rows, gate_all, preferred_element_type=jnp.float32)
    up_proj = jnp.dot(rows, up_all, preferred_element_type=jnp.float32)
    routed = jnp.arange(width) < units
    scale = jnp.where(routed[None, :], row_scale, 1.0)
    hidden = (jax.nn.silu(gate_proj) * up_proj * scale).astype(jnp.bfloat16)
    hidden = hidden_gather(hidden.reshape(n_dp, tok_rows, width))
    hidden = hidden.reshape(4, n_dp * tok_rows, width)
    outputs = jnp.einsum(
        "mtk,mkc->tc",
        hidden,
        down_all.reshape(4, width, down_width),
        preferred_element_type=jnp.float32,
    )
    terms = combine(outputs.astype(jnp.bfloat16).reshape(n_dp, tok_rows, down_width))
    total = stream.reshape(tok_rows, down_width).astype(jnp.float32)
    return (total + jnp.sum(terms.astype(jnp.float32), axis=0)).astype(jnp.bfloat16)


def on_device(
    tree_query,
    new_kv,
    kv_cache,
    page_table,
    cache_len,
    tree_mask,
    out_weight,
    residual_in,
    norm_gain,
    route_ids,
    route_weight,
    w_gate,
    w_up,
    w_down,
    shared_gate,
    shared_up,
    shared_down,
):
    tok_rows = tree_query.shape[0]
    experts = lax.axis_size("dp") * w_gate.shape[0]
    route_count = route_ids.shape[1]
    capacity = min(tok_rows, 4 * tok_rows * route_count // (3 * experts))
    every_row = capacity == tok_rows and w_gate.shape[0] == 1 and lax.axis_size("mp") == 4
    partial_value = attend(
        tree_query,
        new_kv,
        kv_cache,
        page_table,
        cache_len,
        tree_mask,
        out_weight,
        jnp.bfloat16 if every_row else jnp.float32,
    )
    model_width = residual_in.shape[1]
    quarter = model_width // lax.axis_size("mp")
    col_start = lax.axis_index("mp") * quarter
    if every_row:
        return dense_tail(
            partial_value,
            residual_in,
            norm_gain,
            route_ids,
            route_weight,
            w_gate,
            w_up,
            w_down,
            shared_gate,
            shared_up,
            shared_down,
        )
    expert_ids = route_ids.reshape(-1)
    onehot = expert_ids[:, None] == jnp.arange(experts, dtype=jnp.int32)[None, :]
    onehot = onehot.astype(jnp.bfloat16)
    places = jnp.arange(expert_ids.shape[0], dtype=jnp.int32)
    earlier = (places[None, :] < places[:, None]).astype(jnp.bfloat16)
    before = jnp.dot(earlier, onehot, preferred_element_type=jnp.float32)
    slot_index = jnp.sum(before * onehot.astype(jnp.float32), axis=1).astype(jnp.int32)
    targets = (expert_ids * capacity + slot_index).reshape(tok_rows, route_count)
    hits = targets[:, :, None] == jnp.arange(experts * capacity, dtype=jnp.int32)[None, None, :]
    spread = jnp.any(hits, axis=1).astype(jnp.bfloat16)
    gains = jnp.sum(jnp.where(hits, route_weight[:, :, None], 0.0), axis=1)
    summed_heads = lax.psum(partial_value, "mp")
    stream = (residual_in.astype(jnp.float32) + summed_heads).astype(jnp.bfloat16)
    own_stream = lax.dynamic_slice_in_dim(stream, col_start, quarter, 1)
    normed_rows = normalize(stream, norm_gain)
    buffer = lax.dot_general(
        spread, normed_rows, (((0,), (0,)), ((), ())), preferred_element_type=jnp.float32
    ).astype(jnp.bfloat16)
    results = run_experts(
        lax.all_to_all(
            buffer.reshape(experts, capacity, model_width),
            "dp",
            split_axis=0,
            concat_axis=0,
            tiled=True,
        ),
        w_gate,
        w_up,
        w_down,
    )
    shared_out = shared_experts(normed_rows, shared_gate, shared_up, shared_down)
    result_rows = results.reshape(experts * capacity, quarter)
    mixture = jnp.dot(gains, result_rows.astype(jnp.float32), precision=lax.Precision.HIGHEST)
    return (own_stream.astype(jnp.float32) + shared_out.astype(jnp.float32) + mixture).astype(
        jnp.bfloat16
    )


def solution(mesh):
    return jax.shard_map(
        on_device,
        mesh=mesh,
        in_specs=(
            P("dp", "mp"),
            P("dp", None, "mp"),
            P("dp", None, None, "mp"),
            P("dp", None),
            P("dp"),
            P("dp", None, None),
            P("mp", None),
            P("dp", None),
            P(),
            P("dp", None),
            P("dp", None),
            P("dp", None, "mp"),
            P("dp", None, "mp"),
            P("dp", None, "mp"),
            P("dp", "mp"),
            P("dp", "mp"),
            P("mp", "dp"),
        ),
        out_specs=P("dp", "mp"),
        check_vma=False,
    )
```

time: 584 us -> 169 us (0.29)
  waiting for transfers between devices: 262 us -> 0.01 us
  local copies, waits for them, and re-layouts: 167 us -> 6.12 us
  Pallas kernels: 0 us -> 118 us
  blocking collectives: 95.4 us -> 0 us
  starting transfers between devices: 5.82 us -> 21 us
  between operations: 13.7 us -> 0.21 us
  matrix products: 24.5 us -> 18.2 us
    all_gather x4 -> x0, waiting for transfers between devices: 210 us -> none  [the longest x1 64.3 us: shared_experts(): lax.all_gather(shared_gate, 'dp', axis=0, tiled=True)]
    scatter x1 -> x0, local copies, waits for them, and re-layouts: 138 us -> none  [on_device(): buffer.at[expert_ids, slot_index].set(normed_rows[sources])]
    pallas_call x0 -> x4, Pallas kernels: none -> 118 us  [the longest x1 52.6 us: norm_gather(): pl.pallas_call(functools.partial(norm_gather_kernel, n_dp), out_shape=(ja...]
    all_to_all x1 -> x0, blocking collectives: 95.4 us -> none  [on_device(): lax.all_to_all(buffer.at[expert_ids, slot_index].set(normed_rows[sources]...]
    psum x1 -> x0, waiting for transfers between devices: 34 us -> none  [on_device(): summed_heads = lax.psum(partial_value, 'mp')]
    gather x4 -> x0, local copies, waits for them, and re-layouts: 16.8 us -> none  [the longest x2 7.81 us: per_request(): kv_pages = kv_cache[table_row]]
    reduce_scatter x1 -> x0, waiting for transfers between devices: 15.9 us -> none  [shared_experts(): lax.psum_scatter(terms.astype(jnp.bfloat16), 'mp', scatter_dimension=1, t...]
    all_to_all x1 -> x3, starting transfers between devices: 5.48 us -> 21 us  [the longest x1 11.2 us: dense_tail(): lax.all_to_all(by_expert, 'dp', split_axis=0, concat_axis=0, tiled=True)]
  transfers between devices with their start and end apart: 7 -> 3, of which waited for: 6 -> 0; matrix products, arithmetic and copies ran while one was open for 4% -> 9% of each run, Pallas kernels for 0% -> 54%
where the time goes in v1:
time: 169 us; the launch traced here: 168 us
  Pallas kernels  118 us (70%)
  starting transfers between devices  21 us (12%)
  matrix products  18.2 us (11%)
  local copies, waits for them, and re-layouts  6.12 us (4%)
  other arithmetic  5.12 us (3%)
    pallas_call x1, Pallas kernels, norm_gather(): pl.pallas_call(functools.partial(norm_gather_kernel, n_dp), out_shape=(ja...  52.6 us
    pallas_call x1, Pallas kernels, hidden_gather(): pl.pallas_call(functools.partial(hidden_gather_kernel, chunks), out_shape...  34.8 us
    pallas_call x1, Pallas kernels, combine(): pl.pallas_call(functools.partial(combine_kernel, n_dp), out_shape=jax.Sha...  27.4 us
    all_to_all x1, starting transfers between devices, dense_tail(): lax.all_to_all(by_expert, 'dp', split_axis=0, concat_axis=0, tiled=True)  11.2 us
    dot_general x1, matrix products, dense_tail(): up_proj = jnp.dot(rows, up_all, preferred_element_type=jnp.float32)  6.6 us
    dot_general x1, matrix products, dense_tail(): gate_proj = jnp.dot(rows, gate_all, preferred_element_type=jnp.float32)  5.98 us
    all_to_all x1, starting transfers between devices, shared_slices(): parts = lax.all_to_all(parts, 'dp', split_axis=0, concat_axis=0, tiled=True)  5.66 us
    dot_general x1, matrix products, dense_tail(): jnp.einsum('mtk,mkc->tc', hidden, down_all.reshape(4, width, down_width),...  5.59 us
  transfers between devices with their start and end apart: 3, of which 0 were waited for; matrix products, arithmetic and copies ran while one was open for 9% of the time, Pallas kernels for 54%

profile of v1, /device:TPU:13, one launch (start us, length us, event | category | flops | bytes accessed | tf_op | source)
XLA Modules:
  0.0 168.2 jit_solution(14687394763737766230)
XLA Ops:
  0.0 0.0 copy-start
  0.0 0.0 copy-start.3
  0.0 0.0 copy-start.4
  0.0 0.0 copy-start.6
  0.0 0.0 copy-start.7
  0.1 2.4 %pad_maximum_fusion = bf16[8,264,256]{2,1,0:T(8,128)(2,1)} fusion(bf16[8,88,256]{2,1,0:T(8,128)(2,1)} %bitcast.56, bf16[8,88,256]{2,1,0:T(8,128)(2,1)} %bitcast.57, bf16[8,88,256]{2,1,0:T(8,128)(2,1)} %bitcast.58), kind=kLoop, calls=%fused_computation.18 | loop fusion | flops 3244032 | bytes 2162688 | tf_op jit(solution)/shard_map/concatenate | solution.py:389
  2.5 5.7 %all-to-all-start = ((bf16[8,264,256]{2,1,0:T(8,128)(2,1)}), bf16[8,264,256]{2,1,0:T(8,128)(2,1)}, u32[]{:S(2)}, u32[]{:S(2)}) async-start(bf16[8,264,256]{2,1,0:T(8,128)(2,1)} %pad_maximum_fusion), calls=%async_computation | async-start | bytes 2162688 | tf_op jit(solution)/shard_map/all_to_all | solution.py:397
  8.2 0.1 pad.8.clone
  8.3 0.0 copy-start.2
  8.3 1.6 copy-done.2
  9.9 2.8 %attend.1 = bf16[128,2048]{1,0:T(8,128)(2,1)S(1)} custom-call(s32[2,32]{1,0:T(2,128)S(1)} %copy-done.6, s32[2]{0:T(128)S(1)} %copy-done.7, bf16[128,512]{1,0:T(8,128)(2,1)S(1)} %copy-done.3, bf16[128,256]{1,0:T(8,128)(2,1)S(1)} %bitcast.47, s32[2,64,64]{2,1,0:T(8,128)S(1)} %copy-done.4, bf16[40,2,128,128]{3,2,1,0:T(8,128)(2,1)S(1)} %copy-done.1, ...), custom_call_target="tpu_custom_call" | custom-call | flops 1000000000 | bytes 6000000 | tf_op jit(solution)/shard_map/attend/pallas_call | solution.py:101
  12.7 0.0 copy-done
  12.7 0.0 copy-start.12
  12.7 52.6 %norm_gather.1 = (bf16[8,4,32,2048]{3,2,1,0:T(8,128)(2,1)S(1)}, bf16[4,32,512]{2,1,0:T(8,128)(2,1)S(1)}) custom-call(bf16[4,32,2048]{2,1,0:T(8,128)(2,1)S(1)} %bitcast.46, bf16[32,2048]{1,0:T(8,128)(2,1)S(1)} %constant_dynamic-slice_fusion.residual_ref, f32[1,2048]{1,0:T(1,128)S(1)} %bitcast.48), custom_call_target="tpu_custom_call" | custom-call | tf_op jit(solution)/shard_map/norm_gather/pallas_call | solution.py:277
  65.4 2.0 %copy-done.8 = bf16[8,4,32,2048]{3,2,1,0:T(8,128)(2,1)} copy-done((bf16[8,4,32,2048]{3,2,1,0:T(8,128)(2,1)}, bf16[8,4,32,2048]{3,2,1,0:T(8,128)(2,1)S(1)}, u32[]{:S(2)}) %copy-start.8) | copy-done | bytes 4194328
  67.3 0.6 select_reduce_fusion
  67.9 0.0 all-to-all-done
  67.9 11.2 %all-to-all-start.1 = ((f32[8,1,128]{2,1,0:T(1,128)}), f32[8,1,128]{2,1,0:T(1,128)S(1)}, u32[]{:S(2)}, u32[]{:S(2)}) async-start(f32[8,1,128]{2,1,0:T(1,128)} %bitcast.15), calls=%async_computation.1 | async-start | bytes 8192 | tf_op jit(solution)/shard_map/all_to_all | solution.py:438
  79.1 1.3 fusion.26
  80.5 6.0 %fusion = f32[1024,512]{1,0:T(8,128)} fusion(bf16[1024,2048]{1,0:T(8,128)(2,1)} %bitcast.49, bf16[2048,88]{0,1:T(8,128)(2,1)S(1)} %bitcast.55, bf16[2048,352]{0,1:T(8,128)(2,1)S(1)} %bitcast.61, bf16[512]{0:T(512)(128)(2,1)S(1)} %pad.8.clone), kind=kOutput, calls=%fused_computation | convolution fusion | flops 2153775104 | bytes 8094720 | tf_op jit(solution)/shard_map/dot_general | solution.py:449
  86.4 0.1 copy.41
  86.5 0.2 reshape_squeeze.7
  86.7 0.8 copy.48
  87.6 0.0 all-to-all-done.1
  87.6 4.2 %all-to-all-start.2 = ((bf16[4,88,512]{2,1,0:T(8,128)(2,1)}), bf16[4,88,512]{2,1,0:T(8,128)(2,1)S(1)}, u32[]{:S(2)}, u32[]{:S(2)}) async-start(bf16[4,88,512]{2,1,0:T(8,128)(2,1)} %bitcast.44), calls=%async_computation.2 | async-start | bytes 720896 | tf_op jit(solution)/shard_map/all_to_all | solution.py:400
  91.7 6.6 %multiply_convert_fusion = bf16[1024,512]{1,0:T(8,128)(2,1)} fusion(f32[1024,512]{1,0:T(8,128)} %fusion, bf16[1024,2048]{1,0:T(8,128)(2,1)} %bitcast.50, bf16[2048,88]{0,1:T(8,128)(2,1)S(1)} %bitcast.54, bf16[2048,352]{0,1:T(8,128)(2,1)S(1)} %bitcast.62, bf16[512]{0:T(512)(128)(2,1)S(1)} %pad.8.clone, f32[1024]{0:T(1024)S(1)} %bitcast.60, ...), kind=kOutput, calls=%fused_computation.17 | convolution fusion | flops 2157969408 | bytes 9147904 | tf_op jit(solution)/shard_map/dot_general | solution.py:450
  98.4 34.8 %hidden_gather.1 = bf16[4,8,128,512]{3,2,1,0:T(8,128)(2,1)} custom-call(bf16[8,128,512]{2,1,0:T(8,128)(2,1)} %bitcast.52), custom_call_target="tpu_custom_call" | custom-call | tf_op jit(solution)/shard_map/hidden_gather/pallas_call | solution.py:344
  133.1 0.0 all-to-all-done.2
  133.1 5.6 %bitcast_convert_fusion = bf16[1024,512]{1,0:T(8,128)(2,1)} fusion(bf16[4,1024,512]{2,1,0:T(8,128)(2,1)} %bitcast.51, bf16[4,88,512]{2,1,0:T(8,128)(2,1)S(1)} %all-to-all-done.2, bf16[4,352,512]{2,1,0:T(8,128)(2,1)S(1)} %bitcast.63, bf16[512]{0:T(512)(128)(2,1)S(1)} %pad.8.clone), kind=kOutput, calls=%fused_computation.15 | convolution fusion | flops 2154299392 | bytes 7046144 | tf_op jit(solution)/shard_map/mtk,mkc->tc/dot_general | solution.py:456
  138.7 27.4 %combine.1 = bf16[8,128,512]{2,1,0:T(8,128)(2,1)} custom-call(bf16[8,128,512]{2,1,0:T(8,128)(2,1)} %bitcast.53), custom_call_target="tpu_custom_call" | custom-call | tf_op jit(solution)/shard_map/combine/pallas_call | solution.py:374
  166.1 1.4 convert_reduce_fusion
  167.5 0.7 fusion.22
  (26 shorter events, 0.1 us)
Async XLA Ops:
  0.0 12.7 %copy-start = (bf16[128,2048]{1,0:T(8,128)(2,1)S(1)}, bf16[128,2048]{1,0:T(8,128)(2,1)}, u32[]{:S(2)}) copy-start(bf16[128,2048]{1,0:T(8,128)(2,1)} %param.24) | copy-start | bytes 1572868
  0.0 8.1 %copy-start.9 = (bf16[128,2,128]{2,1,0:T(2,128)(2,1)S(1)}, bf16[128,2,128]{2,1,0:T(2,128)(2,1)}, u32[]{:S(2)}) copy-start(bf16[128,2,128]{2,1,0:T(2,128)(2,1)} %param.18) | copy-start | bytes 196612
  0.0 8.2 %copy-start.1 = (bf16[40,2,128,128]{3,2,1,0:T(8,128)(2,1)S(1)}, bf16[40,2,128,128]{3,2,1,0:T(8,128)(2,1)}, u32[]{:S(2)}) copy-start(bf16[40,2,128,128]{3,2,1,0:T(8,128)(2,1)} %cache_ref.1) | copy-start | bytes 7864324
  0.0 8.2 %copy-start.3 = (bf16[128,512]{1,0:T(8,128)(2,1)S(1)}, bf16[128,512]{1,0:T(8,128)(2,1)}, u32[]{:S(2)}) copy-start(bf16[128,512]{1,0:T(8,128)(2,1)} %query_ref.1) | copy-start | bytes 393220
  0.0 8.2 %copy-start.4 = (s32[2,64,64]{2,1,0:T(8,128)S(1)}, s32[2,64,64]{2,1,0:T(8,128)}, u32[]{:S(2)}) copy-start(s32[2,64,64]{2,1,0:T(8,128)} %mask_ref.1) | copy-start | bytes 98308
  0.0 8.2 %copy-start.6 = (s32[2,32]{1,0:T(2,128)S(1)}, s32[2,32]{1,0:T(2,128)}, u32[]{:S(2)}) copy-start(s32[2,32]{1,0:T(2,128)} %table_ref.1) | copy-start | bytes 772
  0.0 8.2 %copy-start.7 = (s32[2]{0:T(128)S(1)}, s32[2]{0:T(128)}, u32[]{:S(2)}) copy-start(s32[2]{0:T(128)} %length_ref.1) | copy-start | bytes 28
  2.5 65.5 %all-to-all-start = ((bf16[8,264,256]{2,1,0:T(8,128)(2,1)}), bf16[8,264,256]{2,1,0:T(8,128)(2,1)}, u32[]{:S(2)}, u32[]{:S(2)}) async-start(bf16[8,264,256]{2,1,0:T(8,128)(2,1)} %pad_maximum_fusion), calls=%async_computation | async-start | bytes 2162688 | tf_op jit(solution)/shard_map/all_to_all | solution.py:397
  8.3 1.6 copy-start.2
  9.9 2.8 %copy-start.5 = (f32[2048]{0:T(1024)S(1)}, f32[2048]{0:T(1024)}, u32[]{:S(2)}) copy-start(f32[2048]{0:T(1024)} %param.25) | copy-start | bytes 24580
  9.9 57.5 %copy-start.10 = (f32[128,6]{0,1:T(8,128)S(1)}, f32[128,6]{0,1:T(8,128)}, u32[]{:S(2)}) copy-start(f32[128,6]{0,1:T(8,128)} %param.27) | copy-start | bytes 9220
  9.9 57.5 %copy-start.11 = (s32[128,6]{0,1:T(8,128)S(1)}, s32[128,6]{0,1:T(8,128)}, u32[]{:S(2)}) copy-start(s32[128,6]{0,1:T(8,128)} %param.26) | copy-start | bytes 9220
  12.7 67.8 %copy-start.12 = (bf16[1,2048,352]{1,2,0:T(8,128)(2,1)S(1)}, bf16[1,2048,352]{1,2,0:T(8,128)(2,1)}, u32[]{:S(2)}) copy-start(bf16[1,2048,352]{1,2,0:T(8,128)(2,1)} %param.28) | copy-start | bytes 4325380
  65.4 2.0 %copy-start.8 = (bf16[8,4,32,2048]{3,2,1,0:T(8,128)(2,1)}, bf16[8,4,32,2048]{3,2,1,0:T(8,128)(2,1)S(1)}, u32[]{:S(2)}) copy-start(bf16[8,4,32,2048]{3,2,1,0:T(8,128)(2,1)S(1)} %get-tuple-element.8) | copy-start | bytes 12582916
  67.9 19.6 %all-to-all-start.1 = ((f32[8,1,128]{2,1,0:T(1,128)}), f32[8,1,128]{2,1,0:T(1,128)S(1)}, u32[]{:S(2)}, u32[]{:S(2)}) async-start(f32[8,1,128]{2,1,0:T(1,128)} %bitcast.15), calls=%async_computation.1 | async-start | bytes 8192 | tf_op jit(solution)/shard_map/all_to_all | solution.py:438
  86.4 5.3 %copy-start.13 = (bf16[1,2048,352]{1,2,0:T(8,128)(2,1)S(1)}, bf16[1,2048,352]{1,2,0:T(8,128)(2,1)}, u32[]{:S(2)}) copy-start(bf16[1,2048,352]{1,2,0:T(8,128)(2,1)} %param.29) | copy-start | bytes 4325380
  87.6 45.5 %all-to-all-start.2 = ((bf16[4,88,512]{2,1,0:T(8,128)(2,1)}), bf16[4,88,512]{2,1,0:T(8,128)(2,1)S(1)}, u32[]{:S(2)}, u32[]{:S(2)}) async-start(bf16[4,88,512]{2,1,0:T(8,128)(2,1)} %bitcast.44), calls=%async_computation.2 | async-start | bytes 720896 | tf_op jit(solution)/shard_map/all_to_all | solution.py:400
  98.3 34.8 %copy-start.14 = (bf16[1,1408,512]{2,1,0:T(8,128)(2,1)S(1)}, bf16[1,1408,512]{2,1,0:T(8,128)(2,1)}, u32[]{:S(2)}) copy-start(bf16[1,1408,512]{2,1,0:T(8,128)(2,1)} %param.30) | copy-start | bytes 4325380

commit v2 on v1

--- a/solution.py
+++ b/solution.py
@@ -307,98 +307,163 @@
     )(partial, residual, gain)
 
 
-def hidden_gather_kernel(
-    chunks, own_ref, all_ref, x_send, x_recv, c_send, c_recv, r_send, r_recv, local_sem
+def expert_kernel(
+    n_dp,
+    units,
+    rows_ref,
+    scale_ref,
+    gate_ref,
+    up_ref,
+    down_ref,
+    terms_ref,
+    hidden,
+    outputs,
+    x_send,
+    x_recv,
+    c_send,
+    c_recv,
+    r_send,
+    r_recv,
+    dp_send,
+    dp_recv,
 ):
     d, m = lax.axis_index("dp"), lax.axis_index("mp")
     core_mate, x_mate, _ = mp_relations(m)
-    greet([(d, core_mate), (d, x_mate)])
-    x_copies = [
-        remote(own_ref.at[k], all_ref.at[m, k], x_send.at[k], x_recv.at[k], (d, x_mate))
-        for k in range(chunks)
-    ]
-    c_copies = [
-        remote(own_ref.at[k], all_ref.at[m, k], c_send.at[k], c_recv.at[k], (d, core_mate))
-        for k in range(chunks)
-    ]
-    for copy in x_copies + c_copies:
-        copy.start()
-    local = pltpu.make_async_copy(own_ref, all_ref.at[m], local_sem)
-    local.start()
-    r_copies = []
-    for k in range(chunks):
-        x_copies[k].wait_recv()
-        block = all_ref.at[x_mate, k]
-        copy = remote(block, block, r_send.at[k], r_recv.at[k], (d, core_mate))
-        copy.start()
-        r_copies.append(copy)
-    local.wait()
-    for copy in x_copies:
-        copy.wait_send()
-    for copy in c_copies + r_copies:
-        copy.wait()
-
-
-def hidden_gather(own):
-    chunks, rows, width = own.shape
+    greet(
+        [(d, core_mate), (d, x_mate)] + [(lax.rem(d + k, n_dp), m) for k in range(1, n_dp)]
+    )
+    relay_lag, finish_lag = 2, 4
+    width = gate_ref.shape[1]
+
+    def block_of(k):
+        return lax.rem(d + k + 1, n_dp)
+
+    def x_copy(k):
+        block = hidden.at[m, block_of(k)]
+        return remote(block, block, x_send.at[k], x_recv.at[k], (d, x_mate))
+
+    def c_copy(k):
+        block = hidden.at[m, block_of(k)]
+        return remote(block, block, c_send.at[k], c_recv.at[k], (d, core_mate))
+
+    def r_copy(k):
+        block = hidden.at[x_mate, block_of(k)]
+        return remote(block, block, r_send.at[k], r_recv.at[k], (d, core_mate))
+
+    def dp_copy(k):
+        t = block_of(k)
+        return remote(outputs.at[t], terms_ref.at[d], dp_send.at[k], dp_recv.at[k], (t, m))
+
+    def step(s, carry):
+        @pl.when(s < n_dp)
+        def _():
+            t = block_of(s)
+            rows = rows_ref[t]
+            gate = jnp.dot(rows, gate_ref[...], preferred_element_type=jnp.float32)
+            up = jnp.dot(rows, up_ref[...], preferred_element_type=jnp.float32)
+            routed = lax.broadcasted_iota(jnp.int32, (1, width), 1) < units
+            scale = jnp.where(routed, scale_ref[t], 1.0)
+            hidden[m, t] = (jax.nn.silu(gate) * up * scale).astype(jnp.bfloat16)
+            x_copy(s).start()
+            c_copy(s).start()
+
+        @pl.when((s >= relay_lag) & (s < n_dp + relay_lag))
+        def _():
+            x_copy(s - relay_lag).wait_recv()
+            r_copy(s - relay_lag).start()
+
+        @pl.when(s >= finish_lag)
+        def _():
+            k = s - finish_lag
+            t = block_of(k)
+            c_copy(k).wait_recv()
+            r_copy(k).wait_recv()
+            total = jnp.dot(hidden[0, t], down_ref[0], preferred_element_type=jnp.float32)
+            for i in range(1, 4):
+                total += jnp.dot(hidden[i, t], down_ref[i], preferred_element_type=jnp.float32)
+            result = total.astype(jnp.bfloat16)
+
+            @pl.when(k < n_dp - 1)
+            def _():
+                outputs[t] = result
+                dp_copy(k).start()
+
+            @pl.when(k == n_dp - 1)
+            def _():
+                terms_ref[d] = result
+
+        return carry
+
+    lax.fori_loop(0, n_dp + finish_lag, step, 0)
+
+    def finish(k, carry):
+        x_copy(k).wait_send()
+        c_copy(k).wait_send()
+        r_copy(k).wait_send()
+
+        @pl.when(k < n_dp - 1)
+        def _():
+            dp_copy(k).wait()
+
+        return carry
+
+    lax.fori_loop(0, n_dp, finish, 0)
+
+
+def run_blocks(units, rows, scale, gate, up, down):
+    n_dp, tok_rows, _ = rows.shape
+    width, columns = gate.shape[1], down.shape[2]
+    vmem, dma = pl.BlockSpec(memory_space=pltpu.VMEM), pltpu.SemaphoreType.DMA
     return pl.pallas_call(
-        functools.partial(hidden_gather_kernel, chunks),
-        out_shape=jax.ShapeDtypeStruct((4, chunks, rows, width), own.dtype),
-        in_specs=[pl.BlockSpec(memory_space=pl.ANY)],
-        out_specs=pl.BlockSpec(memory_space=pl.ANY),
-        scratch_shapes=[pltpu.SemaphoreType.DMA((chunks,))] * 6 + [pltpu.SemaphoreType.DMA],
-        compiler_params=pltpu.CompilerParams(collective_id=1, has_side_effects=True),
-        name="hidden_gather",
-    )(own)
-
-
-def combine_kernel(n_dp, own_ref, all_ref, send, recv, local_sem):
-    d, m = lax.axis_index("dp"), lax.axis_index("mp")
-    peers = [lax.rem(d + k, n_dp) for k in range(1, n_dp)]
-    greet([(peer, m) for peer in peers])
-    copies = [
-        remote(own_ref.at[peers[k]], all_ref.at[d], send.at[k], recv.at[k], (peers[k], m))
-        for k in range(n_dp - 1)
-    ]
-    for copy in copies:
-        copy.start()
-    local = pltpu.make_async_copy(own_ref.at[d], all_ref.at[d], local_sem)
-    local.start()
-    local.wait()
-    for copy in copies:
-        copy.wait()
-
-
-def combine(own):
-    n_dp = own.shape[0]
-    return pl.pallas_call(
-        functools.partial(combine_kernel, n_dp),
-        out_shape=jax.ShapeDtypeStruct(own.shape, own.dtype),
-        in_specs=[pl.BlockSpec(memory_space=pl.ANY)],
-        out_specs=pl.BlockSpec(memory_space=pl.ANY),
-        scratch_shapes=[pltpu.SemaphoreType.DMA((n_dp - 1,))] * 2 + [pltpu.SemaphoreType.DMA],
-        compiler_params=pltpu.CompilerParams(collective_id=2, has_side_effects=True),
-        name="combine",
-    )(own)
-
-
-def shared_slices(shared_gate, shared_up, shared_down):
+        functools.partial(expert_kernel, n_dp, units),
+        out_shape=jax.ShapeDtypeStruct((n_dp, tok_rows, columns), jnp.bfloat16),
+        in_specs=[vmem] * 5,
+        out_specs=vmem,
+        scratch_shapes=[
+            pltpu.VMEM((4, n_dp, tok_rows, width), jnp.bfloat16),
+            pltpu.VMEM((n_dp, tok_rows, columns), jnp.bfloat16),
+        ]
+        + [dma((n_dp,))] * 6
+        + [dma((n_dp - 1,))] * 2,
+        compiler_params=pltpu.CompilerParams(
+            collective_id=1, has_side_effects=True, vmem_limit_bytes=40 * 1024 * 1024
+        ),
+        name="run_blocks",
+    )(rows, scale, gate, up, down)
+
+
+def split_three(values):
+    pieces = []
+    for _ in range(3):
+        piece = lax.reduce_precision(values, 8, 7)
+        pieces.append(piece.astype(jnp.bfloat16))
+        values = values - piece
+    return pieces
+
+
+def shared_slices(shared_gate, shared_up, shared_down, by_expert):
     n_dp = lax.axis_size("dp")
     depth, units = shared_gate.shape
     share = units // n_dp
+    pieces = jnp.stack(split_three(by_expert), axis=1)
+    pieces = jnp.pad(pieces, ((0, 0), (0, 5), (0, depth - pieces.shape[2])))
     parts = jnp.concatenate(
         [
             shared_gate.T.reshape(n_dp, share, depth),
             shared_up.T.reshape(n_dp, share, depth),
             shared_down.reshape(n_dp, share, depth),
+            pieces,
         ],
         axis=1,
     )
     parts = lax.all_to_all(parts, "dp", split_axis=0, concat_axis=0, tiled=True)
-    parts = parts.transpose(1, 0, 2).reshape(3, share, n_dp * depth)
+    row_scale = jnp.sum(
+        parts[:, 3 * share : 3 * share + 3, : by_expert.shape[1]].astype(jnp.float32), axis=1
+    )
+    parts = parts[:, : 3 * share].transpose(1, 0, 2).reshape(3, share, n_dp * depth)
     down = parts[2].reshape(share, 4, -1).transpose(1, 0, 2)
     down = lax.all_to_all(down, "mp", split_axis=0, concat_axis=0, tiled=True)
-    return parts[0].T, parts[1].T, down
+    return parts[0].T, parts[1].T, down, row_scale
 
 
 def dense_tail(
@@ -417,7 +482,11 @@
     n_dp = lax.axis_size("dp")
     tok_rows, model_width = residual_in.shape
     units = w_gate.shape[2]
-    own_gate, own_up, own_down = shared_slices(shared_gate, shared_up, shared_down)
+    chosen = route_ids[None, :, :] == jnp.arange(n_dp, dtype=jnp.int32)[:, None, None]
+    by_expert = jnp.sum(jnp.where(chosen, route_weight[None], 0.0), axis=2)
+    own_gate, own_up, own_down, row_scale = shared_slices(
+        shared_gate, shared_up, shared_down, by_expert
+    )
     share = own_gate.shape[1]
     width = -(-(units + share) // 128) * 128
     spare = width - units - share
@@ -432,11 +501,8 @@
             jnp.zeros((4, spare, down_width), jnp.bfloat16),
         ],
         axis=1,
-    ).reshape(4 * width, down_width)
-    chosen = route_ids[None, :, :] == jnp.arange(n_dp, dtype=jnp.int32)[:, None, None]
-    by_expert = jnp.sum(jnp.where(chosen, route_weight[None], 0.0), axis=2)
-    row_scale = lax.all_to_all(by_expert, "dp", split_axis=0, concat_axis=0, tiled=True)
-    row_scale = row_scale.reshape(n_dp * tok_rows, 1)
+    )
+    row_scale = row_scale.reshape(n_dp, tok_rows, 1)
     slice_rows = tok_rows // 4
     own_start = lax.axis_index("mp") * slice_rows
     rows, stream = norm_gather(
@@ -445,21 +511,8 @@
         lax.dynamic_slice_in_dim(residual_in, own_start, slice_rows, 0),
         norm_gain.reshape(1, model_width),
     )
-    rows = rows.reshape(n_dp * tok_rows, model_width)
-    gate_proj = jnp.dot(rows, gate_all, preferred_element_type=jnp.float32)
-    up_proj = jnp.dot(rows, up_all, preferred_element_type=jnp.float32)
-    routed = jnp.arange(width) < units
-    scale = jnp.where(routed[None, :], row_scale, 1.0)
-    hidden = (jax.nn.silu(gate_proj) * up_proj * scale).astype(jnp.bfloat16)
-    hidden = hidden_gather(hidden.reshape(n_dp, tok_rows, width))
-    hidden = hidden.reshape(4, n_dp * tok_rows, width)
-    outputs = jnp.einsum(
-        "mtk,mkc->tc",
-        hidden,
-        down_all.reshape(4, width, down_width),
-        preferred_element_type=jnp.float32,
-    )
-    terms = combine(outputs.astype(jnp.bfloat16).reshape(n_dp, tok_rows, down_width))
+    rows = rows.reshape(n_dp, tok_rows, model_width)
+    terms = run_blocks(units, rows, row_scale, gate_all, up_all, down_all)
     total = stream.reshape(tok_rows, down_width).astype(jnp.float32)
     return (total + jnp.sum(terms.astype(jnp.float32), axis=0)).astype(jnp.bfloat16)
 

time: 169 us -> 136 us (0.80)
  matrix products: 18.2 us -> 0 us
  Pallas kernels: 118 us -> 100 us
  starting transfers between devices: 21 us -> 9.87 us
  local copies, waits for them, and re-layouts: 6.12 us -> 14.4 us
  other arithmetic: 5.12 us -> 11.3 us
    dot_general x3 -> x0, matrix products: 18.2 us -> none  [the longest x1 6.6 us: dense_tail(): up_proj = jnp.dot(rows, up_all, preferred_element_type=jnp.float32)]
    pallas_call x2 -> x1, Pallas kernels: 62.1 us -> 48.2 us  [run_blocks(): pl.pallas_call(functools.partial(expert_kernel, n_dp, units), out_shape=j...]
    all_to_all x1 -> x0, starting transfers between devices: 11.2 us -> none  [dense_tail(): lax.all_to_all(by_expert, 'dp', split_axis=0, concat_axis=0, tiled=True)]
    unnamed x31 -> x30, local copies, waits for them, and re-layouts: 3.61 us -> 10.3 us
    concatenate x0 -> x2, other arithmetic: none -> 6.58 us  [the longest x1 4.58 us: dense_tail(): up_all = jnp.concatenate([w_up[0], own_up, columns_pad], axis=1)]
    pallas_call x1, Pallas kernels: 52.6 us -> 47.6 us  [norm_gather(): pl.pallas_call(functools.partial(norm_gather_kernel, n_dp), out_shape=(ja...]
  transfers between devices with their start and end apart: 3 -> 2, of which waited for: 0 -> 0; matrix products, arithmetic and copies ran while one was open for 9% -> 8% of each run, Pallas kernels for 54% -> 38%
where the time goes in v2:
time: 136 us
  Pallas kernels  100 us (74%)
  local copies, waits for them, and re-layouts  14.4 us (11%)
  other arithmetic  11.3 us (8%)
  starting transfers between devices  9.87 us (7%)
    pallas_call x1, Pallas kernels, run_blocks(): pl.pallas_call(functools.partial(expert_kernel, n_dp, units), out_shape=j...  48.2 us
    pallas_call x1, Pallas kernels, norm_gather(): pl.pallas_call(functools.partial(norm_gather_kernel, n_dp), out_shape=(ja...  47.6 us
    unnamed x30, local copies, waits for them, and re-layouts  10.3 us
    all_to_all x1, starting transfers between devices, shared_slices(): parts = lax.all_to_all(parts, 'dp', split_axis=0, concat_axis=0, tiled=True)  5.66 us
    concatenate x1, other arithmetic, dense_tail(): up_all = jnp.concatenate([w_up[0], own_up, columns_pad], axis=1)  4.58 us
    all_to_all x1, starting transfers between devices, shared_slices(): down = lax.all_to_all(down, 'mp', split_axis=0, concat_axis=0, tiled=True)  4.21 us
    pallas_call x1, Pallas kernels, attend(): pl.pallas_call(functools.partial(attend_kernel, heads, group, dim ** (-0....  4.2 us
  transfers between devices with their start and end apart: 2, of which 0 were waited for; matrix products, arithmetic and copies ran while one was open for 8% of the time, Pallas kernels for 38%

profile of v2, /device:TPU:13, one launch (start us, length us, event | category | flops | bytes accessed | tf_op | source)
XLA Modules:
  0.0 135.8 jit_solution(13487022914255081679)
XLA Ops:
  0.0 0.8 select_reduce_fusion
  0.8 0.0 copy-start.12
  0.8 0.0 copy-start.11
  0.8 2.4 %fusion.1 = bf16[8,272,256]{2,1,0:T(8,128)(2,1)} fusion(bf16[8,3,128]{2,1,0:T(4,128)(2,1)S(1)} %copy.54, bf16[8,88,256]{2,1,0:T(8,128)(2,1)} %bitcast.48, bf16[8,88,256]{2,1,0:T(8,128)(2,1)} %bitcast.49, bf16[8,88,256]{2,1,0:T(8,128)(2,1)} %bitcast.50), kind=kLoop, calls=%fused_computation.6 | loop fusion | flops 5570560 | bytes 2201600 | tf_op jit(solution)/shard_map/concatenate | solution.py:450
  3.2 5.7 %all-to-all-start = ((bf16[8,272,256]{2,1,0:T(8,128)(2,1)}), bf16[8,272,256]{2,1,0:T(8,128)(2,1)}, u32[]{:S(2)}, u32[]{:S(2)}) async-start(bf16[8,272,256]{2,1,0:T(8,128)(2,1)} %fusion.1), calls=%async_computation | async-start | bytes 2228224 | tf_op jit(solution)/shard_map/all_to_all | solution.py:459
  8.9 1.7 %copy.47 = bf16[1,2048,352]{2,1,0:T(8,128)(2,1)} copy(bf16[1,2048,352]{1,2,0:T(8,128)(2,1)S(1)} %copy-done.11) | data formatting | bytes 2883584 | tf_op args[11]
  10.6 0.0 copy-start.10
  10.6 2.7 %copy.49 = bf16[1,2048,352]{2,1,0:T(8,128)(2,1)} copy(bf16[1,2048,352]{1,2,0:T(8,128)(2,1)} %param.29) | data formatting | bytes 2883584 | tf_op args[12]
  13.3 0.1 pad.13.clone
  13.4 0.0 copy-start.5
  13.4 1.6 %copy-done.5 = bf16[512,2048]{1,0:T(8,128)(2,1)S(1)} copy-done((bf16[512,2048]{1,0:T(8,128)(2,1)S(1)}, bf16[512,2048]{1,0:T(8,128)(2,1)}, u32[]{:S(2)}) %copy-start.5) | copy-done | bytes 2097176
  15.0 4.2 %attend.1 = bf16[128,2048]{1,0:T(8,128)(2,1)S(1)} custom-call(s32[2,32]{1,0:T(2,128)S(1)} %copy-done.9, s32[2]{0:T(128)S(1)} %copy-done.10, bf16[128,512]{1,0:T(8,128)(2,1)S(1)} %copy-done.6, bf16[128,256]{1,0:T(8,128)(2,1)S(1)} %bitcast.41, s32[2,64,64]{2,1,0:T(8,128)S(1)} %copy-done.7, bf16[40,2,128,128]{3,2,1,0:T(8,128)(2,1)S(1)} %copy-done.4, ...), custom_call_target="tpu_custom_call" | custom-call | flops 1000000000 | bytes 6000000 | tf_op jit(solution)/shard_map/attend/pallas_call | solution.py:101
  19.3 47.6 %norm_gather.1 = (bf16[8,4,32,2048]{3,2,1,0:T(8,128)(2,1)S(1)}, bf16[4,32,512]{2,1,0:T(8,128)(2,1)S(1)}) custom-call(bf16[4,32,2048]{2,1,0:T(8,128)(2,1)S(1)} %bitcast.40, bf16[32,2048]{1,0:T(8,128)(2,1)S(1)} %constant_dynamic-slice_fusion.residual_ref, f32[1,2048]{1,0:T(1,128)S(1)} %bitcast.42), custom_call_target="tpu_custom_call" | custom-call | tf_op jit(solution)/shard_map/norm_gather/pallas_call | solution.py:277
  66.9 1.9 %copy-done.2 = bf16[8,4,32,2048]{3,2,1,0:T(8,128)(2,1)} copy-done((bf16[8,4,32,2048]{3,2,1,0:T(8,128)(2,1)}, bf16[8,4,32,2048]{3,2,1,0:T(8,128)(2,1)S(1)}, u32[]{:S(2)}) %copy-start.2) | copy-done | bytes 4194328
  68.8 0.0 all-to-all-done
  68.8 1.3 slice_bitcast_fusion
  70.1 0.1 fusion.5
  70.2 0.1 copy.51
  70.3 0.2 reshape_squeeze.7
  70.5 0.8 copy.58
  71.3 4.2 %all-to-all-start.1 = ((bf16[4,88,512]{2,1,0:T(8,128)(2,1)}), bf16[4,88,512]{2,1,0:T(8,128)(2,1)}, u32[]{:S(2)}, u32[]{:S(2)}) async-start(bf16[4,88,512]{2,1,0:T(8,128)(2,1)} %bitcast.37), calls=%async_computation.1 | async-start | bytes 720896 | tf_op jit(solution)/shard_map/all_to_all | solution.py:465
  75.5 0.3 copy.50
  75.8 1.0 copy.48
  76.8 4.6 %maximum_maximum_fusion.1 = (bf16[2048,512]{1,0:T(8,128)(2,1)S(1)}, bf16[2048,512]{1,0:T(8,128)(2,1)}) fusion(bf16[2048,88]{1,0:T(8,128)(2,1)S(1)} %bitcast.45, bf16[2048,352]{1,0:T(8,128)(2,1)} %bitcast.44, bf16[512]{0:T(512)(128)(2,1)S(1)} %pad.13.clone, bf16[2048,88]{1,0:T(8,128)(2,1)} %bitcast.46, bf16[2048,352]{1,0:T(8,128)(2,1)} %bitcast.43), kind=kLoop, calls=%fused_computation.3 | loop fusion | flops 11534336 | bytes 7799808 | tf_op jit(solution)/shard_map/concatenate | solution.py:495
  81.4 0.7 convert_reduce_fusion.1
  82.1 0.2 copy.53.scale_ref
  82.4 2.0 %maximum_maximum_fusion.2.down_ref = bf16[4,512,512]{2,1,0:T(8,128)(2,1)S(1)} fusion(bf16[4,88,512]{2,1,0:T(8,128)(2,1)} %all-to-all-done.1, bf16[4,352,512]{2,1,0:T(8,128)(2,1)} %bitcast.47, bf16[512]{0:T(512)(128)(2,1)S(1)} %pad.13.clone), kind=kLoop, calls=%fused_computation.4 | loop fusion | flops 6291456 | bytes 3900416 | tf_op jit(solution)/shard_map/concatenate | solution.py:497
  84.4 0.1 copy-done.1
  84.5 2.2 %copy-done.3 = bf16[8,4,32,2048]{3,2,1,0:T(8,128)(2,1)S(1)} copy-done((bf16[8,4,32,2048]{3,2,1,0:T(8,128)(2,1)S(1)}, bf16[8,4,32,2048]{3,2,1,0:T(8,128)(2,1)}, u32[]{:S(2)}) %copy-start.3) | copy-done | bytes 4194328
  86.7 48.2 %run_blocks.1 = bf16[8,128,512]{2,1,0:T(8,128)(2,1)S(1)} custom-call(bf16[8,128,2048]{2,1,0:T(8,128)(2,1)S(1)} %bitcast.39, f32[8,128,1]{2,1,0:T(8,128)S(1)} %copy.53.scale_ref, bf16[2048,512]{1,0:T(8,128)(2,1)S(1)} %copy-done.1, bf16[2048,512]{1,0:T(8,128)(2,1)S(1)} %get-tuple-element.15.up_ref, bf16[4,512,512]{2,1,0:T(8,128)(2,1)S(1)} %maximum_maximum_fusion.2.down_ref), custom_call_target="tpu_custom_call" | custom-call | tf_op jit(solution)/shard_map/run_blocks/pallas_call | solution.py:417
  134.9 0.1 convert_reduce_fusion
  135.1 0.7 fusion.2
  (25 shorter events, 0.1 us)
Async XLA Ops:
  0.0 19.2 %copy-start = (bf16[128,2048]{1,0:T(8,128)(2,1)S(1)}, bf16[128,2048]{1,0:T(8,128)(2,1)}, u32[]{:S(2)}) copy-start(bf16[128,2048]{1,0:T(8,128)(2,1)} %param.24) | copy-start | bytes 1572868
  0.8 8.1 %copy-start.12 = (bf16[128,2,128]{2,1,0:T(2,128)(2,1)S(1)}, bf16[128,2,128]{2,1,0:T(2,128)(2,1)}, u32[]{:S(2)}) copy-start(bf16[128,2,128]{2,1,0:T(2,128)(2,1)} %param.18) | copy-start | bytes 196612
  0.8 8.1 %copy-start.11 = (bf16[1,2048,352]{1,2,0:T(8,128)(2,1)S(1)}, bf16[1,2048,352]{1,2,0:T(8,128)(2,1)}, u32[]{:S(2)}) copy-start(bf16[1,2048,352]{1,2,0:T(8,128)(2,1)} %param.28) | copy-start | bytes 4325380
  3.2 65.6 %all-to-all-start = ((bf16[8,272,256]{2,1,0:T(8,128)(2,1)}), bf16[8,272,256]{2,1,0:T(8,128)(2,1)}, u32[]{:S(2)}, u32[]{:S(2)}) async-start(bf16[8,272,256]{2,1,0:T(8,128)(2,1)} %fusion.1), calls=%async_computation | async-start | bytes 2228224 | tf_op jit(solution)/shard_map/all_to_all | solution.py:459
  10.6 2.8 %copy-start.4 = (bf16[40,2,128,128]{3,2,1,0:T(8,128)(2,1)S(1)}, bf16[40,2,128,128]{3,2,1,0:T(8,128)(2,1)}, u32[]{:S(2)}) copy-start(bf16[40,2,128,128]{3,2,1,0:T(8,128)(2,1)} %cache_ref.1) | copy-start | bytes 7864324
  10.6 2.8 %copy-start.6 = (bf16[128,512]{1,0:T(8,128)(2,1)S(1)}, bf16[128,512]{1,0:T(8,128)(2,1)}, u32[]{:S(2)}) copy-start(bf16[128,512]{1,0:T(8,128)(2,1)} %query_ref.1) | copy-start | bytes 393220
  10.6 2.8 %copy-start.7 = (s32[2,64,64]{2,1,0:T(8,128)S(1)}, s32[2,64,64]{2,1,0:T(8,128)}, u32[]{:S(2)}) copy-start(s32[2,64,64]{2,1,0:T(8,128)} %mask_ref.1) | copy-start | bytes 98308
  10.6 2.8 %copy-start.9 = (s32[2,32]{1,0:T(2,128)S(1)}, s32[2,32]{1,0:T(2,128)}, u32[]{:S(2)}) copy-start(s32[2,32]{1,0:T(2,128)} %table_ref.1) | copy-start | bytes 772
  10.6 2.8 %copy-start.10 = (s32[2]{0:T(128)S(1)}, s32[2]{0:T(128)}, u32[]{:S(2)}) copy-start(s32[2]{0:T(128)} %length_ref.1) | copy-start | bytes 28
  13.4 1.6 %copy-start.5 = (bf16[512,2048]{1,0:T(8,128)(2,1)S(1)}, bf16[512,2048]{1,0:T(8,128)(2,1)}, u32[]{:S(2)}) copy-start(bf16[512,2048]{1,0:T(8,128)(2,1)} %weight_ref.1) | copy-start | bytes 6291460
  15.0 4.2 %copy-start.8 = (f32[2048]{0:T(1024)S(1)}, f32[2048]{0:T(1024)}, u32[]{:S(2)}) copy-start(f32[2048]{0:T(1024)} %param.25) | copy-start | bytes 24580
  66.8 2.0 %copy-start.2 = (bf16[8,4,32,2048]{3,2,1,0:T(8,128)(2,1)}, bf16[8,4,32,2048]{3,2,1,0:T(8,128)(2,1)S(1)}, u32[]{:S(2)}) copy-start(bf16[8,4,32,2048]{3,2,1,0:T(8,128)(2,1)S(1)} %get-tuple-element.8) | copy-start | bytes 12582916
  71.3 11.0 %all-to-all-start.1 = ((bf16[4,88,512]{2,1,0:T(8,128)(2,1)}), bf16[4,88,512]{2,1,0:T(8,128)(2,1)}, u32[]{:S(2)}, u32[]{:S(2)}) async-start(bf16[4,88,512]{2,1,0:T(8,128)(2,1)} %bitcast.37), calls=%async_computation.1 | async-start | bytes 720896 | tf_op jit(solution)/shard_map/all_to_all | solution.py:465
  82.4 2.1 %copy-start.1 = (bf16[2048,512]{1,0:T(8,128)(2,1)S(1)}, bf16[2048,512]{1,0:T(8,128)(2,1)}, u32[]{:S(2)}) copy-start(bf16[2048,512]{1,0:T(8,128)(2,1)} %get-tuple-element.16.gate_ref) | copy-start | bytes 6291460
  84.5 2.2 %copy-start.3 = (bf16[8,4,32,2048]{3,2,1,0:T(8,128)(2,1)S(1)}, bf16[8,4,32,2048]{3,2,1,0:T(8,128)(2,1)}, u32[]{:S(2)}) copy-start(bf16[8,4,32,2048]{3,2,1,0:T(8,128)(2,1)} %copy-done.2) | copy-start | bytes 12582916
